TPU v7x, 32 devices: a whole 2x2x4 slice. The times are simulated.
32 devices in a mesh: gx: 4 (over y, core), gy: 8 (over z, x).
Axes of the slice: x: 2, y: 2, z: 4, core: 2. Of those that a mesh axis runs over, the one named last changes fastest.
Arguments:
- positions: float32 [4, 8, 5, 3, 128], P('gx', 'gy'), may hold values from 0 to 80
- polarity: float32 [4, 8, 5, 128], P('gx', 'gy'), may hold values from 0.25 to 1.25
- direct_field: float32 [4, 8, 5, 6, 128], P('gx', 'gy'), may hold values from -30 to 30
- atom_count: int32 [4, 8, 5], P('gx', 'gy'), may hold values from 64 to 128, as said below
- pair_list: int32 [4, 8, 3, 61], P('gx', 'gy'), may hold values from 0 to 4, as said below
- pair_count: int32 [4, 8], P('gx', 'gy'), may hold values from 9 to 61, as said below
Outputs:
- dipoles: float32 [4, 8, 5, 6, 128], P('gx', 'gy')
- residual: float32 [4, 8, 5, 6, 128], P('gx', 'gy')
Inputs may be any that keep to these rules, and one draw needn't show every extreme that they name: `atom_count`: every device has one block with all 128 atoms. `pair_list`: for e < pair_count the entry (b, s, c) has s in 0..4; with s = 0, c is b or b + 1, otherwise c is b - 1, b or b + 1, all blocks within 0..4; no entry appears twice; every device lists all its s = 0 entries; entries from pair_count on are zeros. `pair_count`: some device lists all 61 possible entries.
All inputs are finite; a program needn't handle non-finite values.
Results may differ from a plain program's by a relative error of at most 0.003.
Values sent between devices are 32-bit elements; how exact they have to be, the bound alone decides.
A program may use at most 64 MiB of HBM per device.

v0:
```python
import jax
import jax.numpy as jnp
from jax import lax
from jax.sharding import PartitionSpec as P

ITERS = 2


thole_factor = 0.39
column_width = 8.0
pair_batch = 8
slot_shift_x = (0.0, 0.0, 1.0, 1.0, 1.0)
slot_shift_y = (0.0, 1.0, -1.0, 0.0, 1.0)


def padded_2(cells, sides, width):
    for axis, dim in sides:
        count = lax.axis_size(axis)
        head = lax.slice_in_dim(cells, 0, width, axis=dim)
        tail = lax.slice_in_dim(cells, cells.shape[dim] - width, cells.shape[dim], axis=dim)
        cells = jnp.concatenate(
            [
                lax.ppermute(tail, axis, [(i, (i + 1) % count) for i in range(count)]),
                cells,
                lax.ppermute(head, axis, [((i + 1) % count, i) for i in range(count)]),
            ],
            axis=dim,
        )
    return cells


def from_behind(value, axis, steps):
    count = lax.axis_size(axis)
    pairs = [(source, (source + steps) % count) for source in range(count)]
    return lax.ppermute(value, axis, pairs)


def tensor_apply(coef_three, coef_five, deltas, moment, axis_sum):
    if axis_sum == 2:
        moments = [moment[:, member, None, :] for member in range(3)]
    else:
        moments = [moment[:, member, :, None] for member in range(3)]
    project = deltas[0] * moments[0] + deltas[1] * moments[1] + deltas[2] * moments[2]
    scaled = coef_five * project
    return jnp.stack(
        [
            jnp.sum(scaled * deltas[member] - coef_three * moments[member], axis=axis_sum)
            for member in range(3)
        ],
        axis=1,
    )


def pair_fields(geom_i, geom_j, dip_i, dip_j, slot_ids, same_block):
    chosen = (slot_ids[:, None] == jnp.arange(5, dtype=jnp.int32)[None, :]).astype(jnp.float32)
    offset_x = column_width * jnp.sum(
        chosen * jnp.array(slot_shift_x, jnp.float32)[None, :], axis=1
    )
    offset_y = column_width * jnp.sum(
        chosen * jnp.array(slot_shift_y, jnp.float32)[None, :], axis=1
    )
    delta_x = geom_j[:, 0, None, :] + offset_x[:, None, None] - geom_i[:, 0, :, None]
    delta_y = geom_j[:, 1, None, :] + offset_y[:, None, None] - geom_i[:, 1, :, None]
    delta_z = geom_j[:, 2, None, :] - geom_i[:, 2, :, None]
    dist_sq = delta_x * delta_x + delta_y * delta_y + delta_z * delta_z
    atom_width = geom_i.shape[2]
    same_atom = jnp.arange(atom_width)[:, None] == jnp.arange(atom_width)[None, :]
    diagonal = same_atom[None, :, :] & same_block[:, None, None]
    dist_sq = jnp.where(diagonal, 1.0, dist_sq)
    inv_dist = lax.rsqrt(dist_sq)
    inv_cube = inv_dist * inv_dist * inv_dist
    root_pol = jnp.sqrt(geom_i[:, 3, :, None] * geom_j[:, 3, None, :])
    damping = thole_factor * dist_sq * jnp.sqrt(dist_sq) / root_pol
    lambda_three = -jnp.expm1(-damping)
    lambda_five = lambda_three - damping * jnp.exp(-damping)
    keep_pair = jnp.where(diagonal, 0.0, 1.0)
    coef_three = keep_pair * lambda_three * inv_cube
    coef_five = keep_pair * 3.0 * lambda_five * inv_cube * inv_dist * inv_dist
    deltas = (delta_x, delta_y, delta_z)
    forward = jnp.concatenate(
        [
            tensor_apply(coef_three, coef_five, deltas, dip_j[:, 0:3], 2),
            tensor_apply(coef_three, coef_five, deltas, dip_j[:, 3:6], 2),
        ],
        axis=1,
    )
    backward = jnp.concatenate(
        [
            tensor_apply(coef_three, coef_five, deltas, dip_i[:, 0:3], 1),
            tensor_apply(coef_three, coef_five, deltas, dip_i[:, 3:6], 1),
        ],
        axis=1,
    )
    return (forward, backward)


def accumulate(geom_stack, dip_stack, entries, pair_total, live_turns, capacity_turns):
    blocks = geom_stack.shape[0] // 5
    atom_width = geom_stack.shape[2]
    targets = jnp.arange(5 * blocks, dtype=jnp.int32)
    padded = jnp.pad(entries, ((0, 0), (0, capacity_turns * pair_batch - entries.shape[1])))

    def one_turn(turn_index, accumulated):
        first_row = (turn_index * pair_batch).astype(jnp.int32)
        group_rows = lax.dynamic_slice_in_dim(padded, first_row, pair_batch, 1)
        own_block = group_rows[0]
        slot_ids = group_rows[1]
        other_block = group_rows[2]
        source = slot_ids * blocks + other_block
        live_rows = (first_row + jnp.arange(pair_batch, dtype=jnp.int32) < pair_total).astype(
            jnp.float32
        )
        same_block = (slot_ids == 0) & (own_block == other_block)
        forward, backward = pair_fields(
            jnp.take(geom_stack, own_block, axis=0),
            jnp.take(geom_stack, source, axis=0),
            jnp.take(dip_stack, own_block, axis=0),
            jnp.take(dip_stack, source, axis=0),
            slot_ids,
            same_block,
        )
        to_own = (own_block[:, None] == targets[None, :]).astype(jnp.float32) * live_rows[:, None]
        twoway = live_rows * (1.0 - same_block.astype(jnp.float32))
        to_other = (source[:, None] == targets[None, :]).astype(jnp.float32) * twoway[:, None]
        accumulated = accumulated + jnp.einsum(
            "gt,gca->tca", to_own, forward, precision=lax.Precision.HIGHEST
        )
        return accumulated + jnp.einsum(
            "gt,gca->tca", to_other, backward, precision=lax.Precision.HIGHEST
        )

    return lax.fori_loop(
        0, live_turns, one_turn, jnp.zeros((5 * blocks, 6, atom_width), jnp.float32)
    )


def neighbours(block_data):
    column = padded_2(block_data[None, None], (("gy", 1),), 1)
    across = from_behind(column, "gx", -1)
    return jnp.concatenate([block_data[None], column[0, 2:3], across[0]], axis=0)


def send_back(partials):
    received = from_behind(partials[None, 1:4], "gx", 1)
    paired = jnp.stack([received[0, 0], received[0, 2] + partials[0]], axis=0)[None]
    column = padded_2(paired, (("gy", 1),), 1)
    return column[0, 0] + column[0, 3] + received[0, 1]


def set_sums(first_vec, second_vec):
    product = (first_vec * second_vec).reshape(first_vec.shape[0], 2, 3, first_vec.shape[2])
    return jnp.sum(product, axis=(0, 2, 3))


def spread_sets(values):
    return jnp.repeat(values, 3)[None, :, None]


def global_sums(local_values):
    return lax.psum(local_values, ("gx", "gy"))


def per_device(positions, polarity, direct_field, atom_count, pair_list, pair_count):
    blocks = positions.shape[2]
    atom_width = positions.shape[4]
    atom_mask = (
        jnp.arange(atom_width, dtype=jnp.int32)[None, :] < atom_count[0, 0][:, None]
    ).astype(jnp.float32)
    pol_wide = polarity[0, 0][:, None, :]
    geometry = jnp.concatenate([positions[0, 0], pol_wide], axis=1)
    entries = pair_list[0, 0]
    pair_total = pair_count[0, 0]
    capacity_turns = -(-entries.shape[1] // pair_batch)
    live_turns = (pair_total + pair_batch - 1) // pair_batch
    residual = direct_field[0, 0] * atom_mask[:, None, :]
    dipoles = jnp.zeros_like(residual)
    geom_stack = None
    search = pol_wide * residual
    rho_now = global_sums(set_sums(residual, search))
    for iteration in range(ITERS):
        operate_geom_stack = geom_stack
        if operate_geom_stack is None:
            stacked = neighbours(jnp.concatenate([geometry, search], axis=1))
            operate_geom_stack = stacked[:, :, 0:4].reshape(5 * blocks, 4, atom_width)
            dip_stack = stacked[:, :, 4:10].reshape(5 * blocks, 6, atom_width)
        else:
            dip_stack = neighbours(search).reshape(5 * blocks, 6, atom_width)
        accumulated = accumulate(
            operate_geom_stack, dip_stack, entries, pair_total, live_turns, capacity_turns
        )
        accumulated = accumulated.reshape(5, blocks, 6, atom_width)
        mutual = (accumulated[0] + send_back(accumulated[1:5])) * atom_mask[:, None, :]
        image_vec = search / pol_wide - mutual
        geom_stack = operate_geom_stack
        step_size = spread_sets(rho_now / global_sums(set_sums(search, image_vec)))
        dipoles = dipoles + step_size * search
        residual = residual - step_size * image_vec
        if iteration + 1 < ITERS:
            precond = pol_wide * residual
            rho_next = global_sums(set_sums(residual, precond))
            search = precond + spread_sets(rho_next / rho_now) * search
            rho_now = rho_next
    return (dipoles[None, None], residual[None, None])


def solution(mesh):
    in_specs = (
        P("gx", "gy", None, None, None),
        P("gx", "gy", None, None),
        P("gx", "gy", None, None, None),
        P("gx", "gy", None),
        P("gx", "gy", None, None),
        P("gx", "gy"),
    )
    out_specs = (P("gx", "gy", None, None, None), P("gx", "gy", None, None, None))
    return jax.shard_map(
        per_device, mesh=mesh, in_specs=in_specs, out_specs=out_specs, check_vma=False
    )
```

profile of v0, /device:TPU:0, one launch (start us, length us, event | category | flops | bytes accessed | tf_op | source)
XLA Modules:
  0.0 321.1 jit_solution(17640803883193026525)
XLA Ops:
  2.8 6.0 %collective-permute-start = (f32[1,1,5,10,128]{4,3,2,1,0:T(8,128)S(1)}, f32[1,1,5,10,128]{4,3,2,1,0:T(8,128)S(1)}, u32[]{:S(2)}, u32[]{:S(2)}) collective-permute-start(f32[1,1,5,10,128]{4,3,2,1,0:T(8,128)S(1)} %get-tuple-element.422), channel_id=1, source_target_pairs={{1,0},{2,1},{3,2},{4,3},{5,4},{6,5},{7,6},{0,7},{9,8},{10,9},{11,1... | collective-permute-start | bytes 76808 | tf_op jit(solution)/shard_map/ppermute | solution.py:25
  10.5 5.0 %collective-permute-done.1 = f32[1,1,5,10,128]{4,3,2,1,0:T(8,128)S(1)} collective-permute-done((f32[1,1,5,10,128]{4,3,2,1,0:T(8,128)S(1)}, f32[1,1,5,10,128]{4,3,2,1,0:T(8,128)S(1)}, u32[]{:S(2)}, u32[]{:S(2)}) %collective-permute-start.1) | collective-permute-done | bytes 25632 | tf_op jit(solution)/shard_map/ppermute | solution.py:23
  18.8 48.5 %while.26 = (s32[]{:T(128)}, f32[25,6,128]{2,0,1:T(8,128)S(1)}, s32[]{:T(128)}, s32[3,64]{1,0:T(4,128)S(1)}, s32[]{:T(128)}, /*index=5*/f32[25,4,128]{2,1,0:T(4,...) while((s32[]{:T(128)}, f32[25,6,128]{2,0,1:T(8,128)S(1)}, ...), condition=%wide.region_18.21_spmd.clone.clone.clone, body=%wide.region_3.20_spmd.sunk.clone.clone.clone.sunk | while | flops 20531916 | bytes 1168975 | solution.py:132
  22.4 2.7 fusion.173
  32.1 2.7 fusion.173
  41.8 2.7 fusion.173
  51.5 2.7 fusion.173
  54.3 1.8 fusion.171
  61.2 2.7 fusion.173
  67.4 23.2 %collective-permute-done.3 = f32[1,3,5,6,128]{4,3,2,1,0:T(8,128)S(1)} collective-permute-done((f32[1,3,5,6,128]{4,3,2,1,0:T(8,128)S(1)}, f32[1,3,5,6,128]{4,3,2,1,0:T(8,128)S(1)}, u32[]{:S(2)}, u32[]{:S(2)}) %collective-permute-start.3) | collective-permute-done | bytes 46112 | tf_op jit(solution)/shard_map/ppermute | solution.py:35
  90.7 4.7 %collective-permute-start.5 = (f32[1,1,5,6,128]{4,3,2,1,0:T(8,128)S(1)}, f32[1,1,5,6,128]{4,3,2,1,0:T(8,128)S(1)}, u32[]{:S(2)}, u32[]{:S(2)}) collective-permute-start(f32[1,1,5,6,128]{4,3,2,1,0:T(8,128)S(1)} %get-tuple-element.419), channel_id=1, source_target_pairs={{1,0},{2,1},{3,2},{4,3},{5,4},{6,5},{7,6},{0,7},{9,8},{10,9},{11,1... | collective-permute-start | bytes 46088 | tf_op jit(solution)/shard_map/ppermute | solution.py:25
  97.2 3.1 collective-permute-done.5
  100.8 41.6 %all-reduce.1 = (f32[2]{0:T(128)S(1)}, f32[2]{0:T(128)S(1)}) all-reduce(f32[2]{0:T(128)S(1)} %reduce_sum.318, f32[2]{0:T(128)S(1)} %reduce_sum.321), channel_id=1, replica_groups=mesh['gx'=4,'gy'=8] {'gx','gy'}, use_global_device_ids=true, to_apply=%region_2.3 | all-reduce | flops 4 | bytes 32 | tf_op jit(solution)/shard_map/psum | solution.py:160
  143.0 39.0 %psum.30 = f32[2]{0:T(128)S(1)} all-reduce(f32[2]{0:T(128)S(1)} %reduce_sum.324), channel_id=1, replica_groups=mesh['gx'=4,'gy'=8] {'gx','gy'}, use_global_device_ids=true, to_apply=%region_24.27 | all-reduce | flops 2 | bytes 16 | tf_op jit(solution)/shard_map/psum | solution.py:160
  182.3 3.3 %collective-permute-start.6 = (f32[1,1,5,6,128]{4,3,2,1,0:T(8,128)S(1)}, f32[1,1,5,6,128]{4,3,2,1,0:T(8,128)S(1)}, u32[]{:S(2)}, u32[]{:S(2)}) collective-permute-start(f32[1,1,5,6,128]{4,3,2,1,0:T(8,128)S(1)} %multiply_add_fusion), channel_id=1, source_target_pairs={{1,0},{2,1},{3,2},{4,3},{5,4},{6,5},{7,6},{0,7},{9,8},{10,9},{11,1... | collective-permute-start | bytes 46088 | tf_op jit(solution)/shard_map/ppermute | solution.py:25
  187.0 5.0 %collective-permute-done.7 = f32[1,1,5,6,128]{4,3,2,1,0:T(8,128)S(1)} collective-permute-done((f32[1,1,5,6,128]{4,3,2,1,0:T(8,128)S(1)}, f32[1,1,5,6,128]{4,3,2,1,0:T(8,128)S(1)}, u32[]{:S(2)}, u32[]{:S(2)}) %collective-permute-start.7) | collective-permute-done | bytes 15392 | tf_op jit(solution)/shard_map/ppermute | solution.py:23
  192.2 1.8 collective-permute-done.8
  194.0 48.6 %while.27 = (s32[]{:T(128)}, f32[25,6,128]{2,0,1:T(8,128)S(1)}, s32[]{:T(128)}, s32[3,64]{1,0:T(4,128)S(1)}, s32[]{:T(128)}, /*index=5*/f32[25,4,128]{2,1,0:T(4,...) while((s32[]{:T(128)}, f32[25,6,128]{2,0,1:T(8,128)S(1)}, ...), condition=%wide.region_40.43_spmd.clone.clone.clone, body=%wide.region_25.42_spmd.sunk.clone.clone.clone.sunk | while | flops 20531916 | bytes 1168975 | solution.py:132
  197.7 2.8 fusion.182
  200.5 1.8 fusion.180
  207.4 2.8 fusion.182
  210.2 1.8 fusion.180
  217.1 2.8 fusion.182
  220.0 1.8 fusion.180
  226.9 2.8 fusion.182
  229.7 1.8 fusion.180
  236.6 2.8 fusion.182
  239.4 1.8 fusion.180
  242.8 23.1 %collective-permute-done.9 = f32[1,3,5,6,128]{4,3,2,1,0:T(8,128)S(1)} collective-permute-done((f32[1,3,5,6,128]{4,3,2,1,0:T(8,128)S(1)}, f32[1,3,5,6,128]{4,3,2,1,0:T(8,128)S(1)}, u32[]{:S(2)}, u32[]{:S(2)}) %collective-permute-start.9) | collective-permute-done | bytes 46112 | tf_op jit(solution)/shard_map/ppermute | solution.py:35
  266.0 4.7 %collective-permute-start.11 = (f32[1,1,5,6,128]{4,3,2,1,0:T(8,128)S(1)}, f32[1,1,5,6,128]{4,3,2,1,0:T(8,128)S(1)}, u32[]{:S(2)}, u32[]{:S(2)}) collective-permute-start(f32[1,1,5,6,128]{4,3,2,1,0:T(8,128)S(1)} %get-tuple-element.417), channel_id=1, source_target_pairs={{1,0},{2,1},{3,2},{4,3},{5,4},{6,5},{7,6},{0,7},{9,8},{10,9},{11,1... | collective-permute-start | bytes 46088 | tf_op jit(solution)/shard_map/ppermute | solution.py:25
  272.5 5.2 %collective-permute-done.11 = f32[1,1,5,6,128]{4,3,2,1,0:T(8,128)S(1)} collective-permute-done((f32[1,1,5,6,128]{4,3,2,1,0:T(8,128)S(1)}, f32[1,1,5,6,128]{4,3,2,1,0:T(8,128)S(1)}, u32[]{:S(2)}, u32[]{:S(2)}) %collective-permute-start.11) | collective-permute-done | bytes 15392 | tf_op jit(solution)/shard_map/ppermute | solution.py:25
  278.0 41.6 %psum.31 = f32[2]{0:T(128)S(1)} all-reduce(f32[2]{0:T(128)S(1)} %reduce_sum.327), channel_id=1, replica_groups=mesh['gx'=4,'gy'=8] {'gx','gy'}, use_global_device_ids=true, to_apply=%region_43.46 | all-reduce | flops 2 | bytes 16 | tf_op jit(solution)/shard_map/psum | solution.py:160
  (430 shorter events, 71.4 us)
Async XLA Ops:
  0.6 1.4 copy-start.4
  0.6 1.4 copy-start
  2.1 0.7 copy-start.3
  2.8 7.7 %collective-permute-start = (f32[1,1,5,10,128]{4,3,2,1,0:T(8,128)S(1)}, f32[1,1,5,10,128]{4,3,2,1,0:T(8,128)S(1)}, u32[]{:S(2)}, u32[]{:S(2)}) collective-permute-start(f32[1,1,5,10,128]{4,3,2,1,0:T(8,128)S(1)} %get-tuple-element.422), channel_id=1, source_target_pairs={{1,0},{2,1},{3,2},{4,3},{5,4},{6,5},{7,6},{0,7},{9,8},{10,9},{11,1... | collective-permute-start | bytes 76808 | tf_op jit(solution)/shard_map/ppermute | solution.py:25
  8.8 6.7 %collective-permute-start.1 = (f32[1,1,5,10,128]{4,3,2,1,0:T(8,128)S(1)}, f32[1,1,5,10,128]{4,3,2,1,0:T(8,128)S(1)}, u32[]{:S(2)}, u32[]{:S(2)}) collective-permute-start(f32[1,1,5,10,128]{4,3,2,1,0:T(8,128)S(1)} %get-tuple-element.422), channel_id=1, source_target_pairs={{0,1},{1,2},{2,3},{3,4},{4,5},{5,6},{6,7},{7,0},{8,9},{9,10},{10,1... | collective-permute-start | bytes 76808 | tf_op jit(solution)/shard_map/ppermute | solution.py:23
  15.5 2.5 collective-permute-start.2
  16.3 0.7 copy-start.5
  18.1 0.7 copy-start.1
  18.1 0.7 copy-start.2
  67.4 23.2 %collective-permute-start.3 = (f32[1,3,5,6,128]{4,3,2,1,0:T(8,128)S(1)}, f32[1,3,5,6,128]{4,3,2,1,0:T(8,128)S(1)}, u32[]{:S(2)}, u32[]{:S(2)}) collective-permute-start(f32[1,3,5,6,128]{4,3,2,1,0:T(8,128)S(1)} %bitcast.454), channel_id=1, source_target_pairs={{0,8},{8,16},{16,24},{24,0},{1,9},{9,17},{17,25},{25,1},{2,10},{10... | collective-permute-start | bytes 138248 | tf_op jit(solution)/shard_map/ppermute | solution.py:35
  90.6 6.5 %collective-permute-start.4 = (f32[1,1,5,6,128]{4,3,2,1,0:T(8,128)S(1)}, f32[1,1,5,6,128]{4,3,2,1,0:T(8,128)S(1)}, u32[]{:S(2)}, u32[]{:S(2)}) collective-permute-start(f32[1,1,5,6,128]{4,3,2,1,0:T(8,128)S(1)} %get-tuple-element.420), channel_id=1, source_target_pairs={{0,1},{1,2},{2,3},{3,4},{4,5},{5,6},{6,7},{7,0},{8,9},{9,10},{10,1... | collective-permute-start | bytes 46088 | tf_op jit(solution)/shard_map/ppermute | solution.py:23
  90.7 9.5 %collective-permute-start.5 = (f32[1,1,5,6,128]{4,3,2,1,0:T(8,128)S(1)}, f32[1,1,5,6,128]{4,3,2,1,0:T(8,128)S(1)}, u32[]{:S(2)}, u32[]{:S(2)}) collective-permute-start(f32[1,1,5,6,128]{4,3,2,1,0:T(8,128)S(1)} %get-tuple-element.419), channel_id=1, source_target_pairs={{1,0},{2,1},{3,2},{4,3},{5,4},{6,5},{7,6},{0,7},{9,8},{10,9},{11,1... | collective-permute-start | bytes 46088 | tf_op jit(solution)/shard_map/ppermute | solution.py:25
  182.3 4.8 %collective-permute-start.6 = (f32[1,1,5,6,128]{4,3,2,1,0:T(8,128)S(1)}, f32[1,1,5,6,128]{4,3,2,1,0:T(8,128)S(1)}, u32[]{:S(2)}, u32[]{:S(2)}) collective-permute-start(f32[1,1,5,6,128]{4,3,2,1,0:T(8,128)S(1)} %multiply_add_fusion), channel_id=1, source_target_pairs={{1,0},{2,1},{3,2},{4,3},{5,4},{6,5},{7,6},{0,7},{9,8},{10,9},{11,1... | collective-permute-start | bytes 46088 | tf_op jit(solution)/shard_map/ppermute | solution.py:25
  185.6 6.5 %collective-permute-start.7 = (f32[1,1,5,6,128]{4,3,2,1,0:T(8,128)S(1)}, f32[1,1,5,6,128]{4,3,2,1,0:T(8,128)S(1)}, u32[]{:S(2)}, u32[]{:S(2)}) collective-permute-start(f32[1,1,5,6,128]{4,3,2,1,0:T(8,128)S(1)} %multiply_add_fusion), channel_id=1, source_target_pairs={{0,1},{1,2},{2,3},{3,4},{4,5},{5,6},{6,7},{7,0},{8,9},{9,10},{10,1... | collective-permute-start | bytes 46088 | tf_op jit(solution)/shard_map/ppermute | solution.py:23
  192.1 1.9 collective-permute-start.8
  242.7 23.2 %collective-permute-start.9 = (f32[1,3,5,6,128]{4,3,2,1,0:T(8,128)S(1)}, f32[1,3,5,6,128]{4,3,2,1,0:T(8,128)S(1)}, u32[]{:S(2)}, u32[]{:S(2)}) collective-permute-start(f32[1,3,5,6,128]{4,3,2,1,0:T(8,128)S(1)} %bitcast.455), channel_id=1, source_target_pairs={{0,8},{8,16},{16,24},{24,0},{1,9},{9,17},{17,25},{25,1},{2,10},{10... | collective-permute-start | bytes 138248 | tf_op jit(solution)/shard_map/ppermute | solution.py:35
  266.0 6.5 %collective-permute-start.10 = (f32[1,1,5,6,128]{4,3,2,1,0:T(8,128)S(1)}, f32[1,1,5,6,128]{4,3,2,1,0:T(8,128)S(1)}, u32[]{:S(2)}, u32[]{:S(2)}) collective-permute-start(f32[1,1,5,6,128]{4,3,2,1,0:T(8,128)S(1)} %get-tuple-element.418), channel_id=1, source_target_pairs={{0,1},{1,2},{2,3},{3,4},{4,5},{5,6},{6,7},{7,0},{8,9},{9,10},{10,1... | collective-permute-start | bytes 46088 | tf_op jit(solution)/shard_map/ppermute | solution.py:23
  266.0 11.6 %collective-permute-start.11 = (f32[1,1,5,6,128]{4,3,2,1,0:T(8,128)S(1)}, f32[1,1,5,6,128]{4,3,2,1,0:T(8,128)S(1)}, u32[]{:S(2)}, u32[]{:S(2)}) collective-permute-start(f32[1,1,5,6,128]{4,3,2,1,0:T(8,128)S(1)} %get-tuple-element.417), channel_id=1, source_target_pairs={{1,0},{2,1},{3,2},{4,3},{5,4},{6,5},{7,6},{0,7},{9,8},{10,9},{11,1... | collective-permute-start | bytes 46088 | tf_op jit(solution)/shard_map/ppermute | solution.py:25
where the time goes:
time: 327 us; the launch traced here: 321 us
  blocking collectives  122 us (37%)
  waiting for transfers between devices  74.1 us (23%)
  other arithmetic  65.1 us (20%)
  local copies, waits for them, and re-layouts  29.2 us (9%)
  starting transfers between devices  19.1 us (6%)
  matrix products  7.15 us (2%)
    psum x3, blocking collectives, global_sums(): return lax.psum(local_values, ('gx', 'gy'))  122 us
    ppermute x4, waiting for transfers between devices, from_behind(): return lax.ppermute(value, axis, pairs)  49.2 us
    reduce_sum x20, other arithmetic, tensor_apply(): jnp.sum(scaled * deltas[member] - coef_three * moments[member], axis=axis...  45.1 us
    ppermute x4, starting transfers between devices, padded_2(): lax.ppermute(head, axis, [((i + 1) % count, i) for i in range(count)])  18.7 us
    ppermute x4, waiting for transfers between devices, padded_2(): lax.ppermute(tail, axis, [(i, (i + 1) % count) for i in range(count)])  13.5 us
    ppermute x4, waiting for transfers between devices, padded_2(): lax.ppermute(head, axis, [((i + 1) % count, i) for i in range(count)])  11.4 us
    mul x10, other arithmetic, one_turn(): twoway = live_rows * (1.0 - same_block.astype(jnp.float32))  6.54 us
  transfers between devices with their start and end apart: 12, of which 12 were waited for; matrix products, arithmetic and copies ran while one was open for 0% of the time, Pallas kernels for 0%

commit v1 on v0

v1 whole, which is shorter than its diff:
```python
import functools

import jax
import jax.numpy as jnp
from jax import lax
from jax.experimental import pallas as pl
from jax.experimental.pallas import tpu as pltpu
from jax.sharding import PartitionSpec as P

thole_factor = 0.39
column_width = 8.0
slot_moves = ((0, 1), (1, -1), (1, 0), (1, 1))
GEO_ROWS = 24
ROWS = 16
MESH = pl.DeviceIdType.MESH


def kernel(
    nx,
    ny,
    blocks,
    count_ref,
    total_ref,
    pos_ref,
    pol_ref,
    field_ref,
    list_ref,
    dip_ref,
    res_ref,
    mail,
    geo,
    vrow2,
    vhalo2,
    gmail,
    polw,
    maskw,
    resid,
    image,
    weight,
    gb,
    vb,
    fa,
    bacc,
    bown,
    tens,
    tdiag,
    toff,
    back_out,
    back_in,
    ar_out,
    arx,
    ary,
    mail_ss,
    mail_rs,
    back_ss,
    back_rs,
    arx_ss,
    arx_rs,
    ary_ss,
    ary_rs,
):
    atoms = pos_ref.shape[2]
    groups = atoms // ROWS
    comps = 6 * blocks
    vrows = polw.shape[0]
    me_x, me_y = lax.axis_index("gx"), lax.axis_index("gy")

    def device(dx, dy):
        return (lax.rem(me_x + (dx % nx), nx), lax.rem(me_y + (dy % ny), ny))

    partners = {((a * dx) % nx, (a * dy) % ny) for dx, dy in slot_moves for a in (1, -1)}
    partners |= {(d, 0) for d in range(1, nx)} | {(0, d) for d in range(1, ny)}
    partners = sorted(partners - {(0, 0)})
    barrier = pltpu.get_barrier_semaphore()
    for dx, dy in partners:
        pl.semaphore_signal(barrier, inc=1, device_id=device(dx, dy), device_id_type=MESH)

    lane = lax.broadcasted_iota(jnp.int32, (1, atoms), 1)
    mail[...] = jnp.zeros_like(mail)
    vrow2[...] = jnp.zeros_like(vrow2)
    polw[...] = jnp.ones_like(polw)
    maskw[...] = jnp.zeros_like(maskw)
    resid[...] = jnp.zeros_like(resid)
    for b in range(blocks):
        mask = (lane < count_ref[0, b]).astype(jnp.float32)
        pol = pol_ref[pl.ds(b, 1), :]
        mail[pl.ds(4 * b, 3), :] = pos_ref[b]
        mail[pl.ds(4 * b + 3, 1), :] = (thole_factor**0.5) * lax.rsqrt(pol)
        own = field_ref[b] * mask
        resid[pl.ds(6 * b, 6), :] = own
        mail[pl.ds(GEO_ROWS + 6 * b, 6), :] = own * pol
        polw[pl.ds(6 * b, 6), :] = jnp.broadcast_to(pol, (6, atoms))
        maskw[pl.ds(6 * b, 6), :] = jnp.broadcast_to(mask, (6, atoms))

    pl.semaphore_wait(barrier, len(partners))

    def send_mail(turn, source, target):
        copies = []
        for s, (dx, dy) in enumerate(slot_moves):
            copy = pltpu.make_async_remote_copy(
                src_ref=source,
                dst_ref=target.at[s],
                send_sem=mail_ss.at[turn, s],
                recv_sem=mail_rs.at[turn, s],
                device_id=device(-dx, -dy),
                device_id_type=MESH,
            )
            copy.start()
            copies.append(copy)
        return copies

    def send_back(turn):
        copies = []
        for s, (dx, dy) in enumerate(slot_moves):
            back_out[turn, s, pl.ds(0, comps), :] = jnp.sum(bacc[s], axis=1)
            copy = pltpu.make_async_remote_copy(
                src_ref=back_out.at[turn, s],
                dst_ref=back_in.at[turn, s],
                send_sem=back_ss.at[turn, s],
                recv_sem=back_rs.at[turn, s],
                device_id=device(dx, dy),
                device_id_type=MESH,
            )
            copy.start()
            copies.append(copy)
        return copies

    def spread_x(turn):
        copies = []
        for d in range(1, nx):
            copy = pltpu.make_async_remote_copy(
                src_ref=ar_out.at[turn, 0],
                dst_ref=arx.at[turn, d - 1],
                send_sem=arx_ss.at[turn, d - 1],
                recv_sem=arx_rs.at[turn, d - 1],
                device_id=device(d, 0),
                device_id_type=MESH,
            )
            copy.start()
            copies.append(copy)
        return copies

    def spread_y(turn):
        copies = []
        for d in range(1, ny):
            copy = pltpu.make_async_remote_copy(
                src_ref=ar_out.at[turn, 1],
                dst_ref=ary.at[turn, d - 1],
                send_sem=ary_ss.at[turn, d - 1],
                recv_sem=ary_rs.at[turn, d - 1],
                device_id=device(0, d),
                device_id_type=MESH,
            )
            copy.start()
            copies.append(copy)
        return copies

    started = []
    row_id = lax.broadcasted_iota(jnp.int32, (vrows, atoms), 0)
    in_set_d = lax.rem(row_id, 6) < 3

    def reduce_start(turn, products):
        parts = []
        for prod in products:
            d_part = jnp.where(in_set_d, prod, 0.0)
            parts.append(jnp.sum(d_part, axis=0, keepdims=True))
            parts.append(jnp.sum(prod - d_part, axis=0, keepdims=True))
        parts.append(jnp.zeros((8 - len(parts), atoms), jnp.float32))
        ar_out[turn, 0] = jnp.concatenate(parts, axis=0)
        copies = spread_x(turn)
        started.extend(copies)
        return copies

    def reduce_middle(turn, copies):
        total = ar_out[turn, 0]
        for d, copy in enumerate(copies):
            copy.wait_recv()
            total = total + arx[turn, d]
        ar_out[turn, 1] = total
        copies = spread_y(turn)
        started.extend(copies)
        return copies

    def reduce_end(turn, copies):
        total = ar_out[turn, 1]
        for d, copy in enumerate(copies):
            copy.wait_recv()
            total = total + ary[turn, d]
        return jnp.sum(total, axis=1, keepdims=True)

    def spread_sets(first, second):
        wide = jnp.broadcast_to(first, (vrows, atoms))
        return jnp.where(in_set_d, wide, jnp.broadcast_to(second, (vrows, atoms)))

    def broadcast_rows(rows, target, count):
        square = jnp.concatenate(
            [rows, jnp.zeros((atoms - rows.shape[0], atoms), jnp.float32)], axis=0
        ).T
        for r in range(count):
            target[r] = jnp.broadcast_to(square[:, r : r + 1], (atoms, atoms))

    def tensor(own, other, keep, diagonal):
        dx, dy, dz = other[0] - own[0], other[1] - own[1], other[2] - own[2]
        dist_sq = dx * dx + dy * dy + dz * dz
        if diagonal is not None:
            dist_sq = jnp.where(diagonal, 1.0, dist_sq)
        inv = lax.rsqrt(dist_sq)
        inv_sq = inv * inv
        damping = dist_sq * dist_sq * inv * (own[3] * other[3])
        decay = jnp.exp(-damping)
        l3 = 1.0 - decay
        l5 = l3 - damping * decay
        level = 3.0 * l5 * inv
        root = level * lax.rsqrt(level) * inv_sq
        c3 = l3 * (inv_sq * inv)
        if keep is not None:
            root = root * keep
            c3 = c3 * keep
        if diagonal is not None:
            root = jnp.where(diagonal, 0.0, root)
            c3 = jnp.where(diagonal, 0.0, c3)
        return root * dx, root * dy, root * dz, c3

    def apply(t, v):
        out = []
        for k in (0, 3):
            project = t[0] * v[k] + t[1] * v[k + 1] + t[2] * v[k + 2]
            out += [t[m] * project - t[3] * v[k + m] for m in range(3)]
        return out

    def fold(x):
        return x[0:8] + x[8:16]

    def rows_of(ref, first, count):
        return [ref[pl.ds(first + m, 1), :] for m in range(count)]

    def own_part(ref, first, g, count):
        return [ref[first + m, pl.ds(g * ROWS, ROWS), :] for m in range(count)]

    def diag_pairs(turn, vref, voff):
        def step(n, carry):
            b, g = n // groups, lax.rem(n, groups)
            if turn == 0:
                row = g * ROWS + lax.broadcasted_iota(jnp.int32, (ROWS, atoms), 0)
                col = lax.broadcasted_iota(jnp.int32, (ROWS, atoms), 1)
                t = tensor(
                    own_part(gb, 4 * b, g, 4), rows_of(mail, 4 * b, 4), None, row == col
                )
                for m in range(4):
                    tdiag[n, m] = t[m]
            else:
                t = [tdiag[n, m] for m in range(4)]
            out = apply(t, rows_of(vref, voff + 6 * b, 6))
            for m in range(6):
                fa[6 * b + m, pl.ds(g * ROWS, ROWS), :] = out[m]
            return carry

        lax.fori_loop(0, blocks * groups, step, 0)

    def off_pairs(turn, vref, voff):
        bown[...] = jnp.zeros_like(bown)

        def step(n, carry):
            b, g = n // groups, lax.rem(n, groups)
            if turn == 0:
                t = tensor(
                    own_part(gb, 4 * b, g, 4), rows_of(mail, 4 * b + 4, 4), None, None
                )
                for m in range(4):
                    toff[n, m] = t[m]
            else:
                t = [toff[n, m] for m in range(4)]
            out = apply(t, rows_of(vref, voff + 6 * b + 6, 6))
            ret = apply(t, own_part(vb, 6 * b, g, 6))
            for m in range(6):
                fa[6 * b + m, pl.ds(g * ROWS, ROWS), :] += out[m]
                bown[6 * b + 6 + m] += fold(ret[m])
            return carry

        lax.fori_loop(0, (blocks - 1) * groups, step, 0)

    def halo_pairs(turn, vhalo, voff, first, last):
        def step(n, carry):
            k, g = n // groups, lax.rem(n, groups)
            b = (k + 1) // 3
            c = k - 2 * b
            vi = own_part(vb, 6 * b, g, 6)
            if turn == 0:
                own = own_part(gb, 4 * b, g, 4)
            total = None
            for s in range(4):
                if turn == 0:
                    keep = weight[pl.ds((s + 1) * blocks * blocks + b * blocks + c, 1), :]
                    other = [geo[s, pl.ds(4 * c + m, 1), :] for m in range(4)]
                    t = tensor(own, other, keep, None)
                    for m in range(4):
                        tens[n, s, m] = t[m]
                else:
                    t = [tens[n, s, m] for m in range(4)]
                vj = [vhalo[s, pl.ds(voff + 6 * c + m, 1), :] for m in range(6)]
                out = apply(t, vj)
                total = out if total is None else [p + q for p, q in zip(total, out)]
                ret = apply(t, vi)
                for m in range(6):
                    bacc[s, 6 * c + m] += fold(ret[m])
            for m in range(6):
                fa[6 * b + m, pl.ds(g * ROWS, ROWS), :] += total[m]
            return carry

        lax.fori_loop(first * groups, last * groups, step, 0)

    lane_sq = lax.broadcasted_iota(jnp.int32, (atoms, atoms), 1)

    def own_field():
        square = jnp.zeros((atoms, atoms), jnp.float32)
        for r in range(comps):
            square = jnp.where(lane_sq == r, jnp.sum(fa[r], axis=1, keepdims=True), square)
        image[...] = jnp.zeros_like(image)
        image[pl.ds(0, comps), :] = jnp.sum(bown[...], axis=1)
        return square.T[0:vrows] + image[...]

    links = 3 * blocks - 2
    own_vec = mail.at[pl.ds(GEO_ROWS, vrows)]

    mails = send_mail(0, mail, gmail)
    started.extend(mails)
    back_out[...] = jnp.zeros_like(back_out)
    search = own_vec[...]
    first_res = resid[...]
    broadcast_rows(mail[pl.ds(0, GEO_ROWS), :], gb, 4 * blocks)
    broadcast_rows(search, vb, comps)
    entry = list_ref[...]
    code = (entry[1:2] * blocks + entry[0:1]) * blocks + entry[2:3]
    here = lax.broadcasted_iota(jnp.int32, code.shape, 1) < total_ref[0, 0]
    code = jnp.where(here, code, -1)
    names = lax.broadcasted_iota(jnp.int32, (weight.shape[0], code.shape[1]), 0)
    found = jnp.sum((names == code).astype(jnp.float32), axis=1, keepdims=True)
    weight[...] = jnp.broadcast_to(found, weight.shape)

    bacc[...] = jnp.zeros_like(bacc)
    diag_pairs(0, mail, GEO_ROWS)
    geo_row = lax.rem(lax.broadcasted_iota(jnp.int32, (GEO_ROWS, atoms), 0), 4)
    for s, (dx, dy) in enumerate(slot_moves):
        mails[s].wait_recv()
        shift = jnp.where(geo_row == 0, column_width * dx, 0.0)
        shift = jnp.where(geo_row == 1, column_width * dy, shift)
        geo[s] = gmail[s, pl.ds(0, GEO_ROWS), :] + shift
    halo_pairs(0, gmail, GEO_ROWS, 0, links)
    backs = send_back(0)
    started.extend(backs)
    off_pairs(0, mail, GEO_ROWS)
    mutual = own_field()
    for s in range(4):
        backs[s].wait_recv()
        mutual = mutual + back_in[0, s]
    image_one = search / polw[...] - mutual * maskw[...]
    vec_two = polw[...] * image_one
    vrow2[...] = vec_two

    mails = send_mail(1, vrow2, vhalo2)
    started.extend(mails)
    sums = reduce_start(0, (first_res * search, search * image_one))
    broadcast_rows(vec_two, vb, comps)
    bacc[...] = jnp.zeros_like(bacc)
    diag_pairs(1, vrow2, 0)
    for s in range(4):
        mails[s].wait_recv()
    cuts = [links * i // 5 for i in range(6)]
    halo_pairs(1, vhalo2, 0, cuts[0], cuts[1])
    sums = reduce_middle(0, sums)
    halo_pairs(1, vhalo2, 0, cuts[1], cuts[2])
    total = reduce_end(0, sums)
    rho_d, rho_p = total[0:1], total[1:2]
    step_one = spread_sets(rho_d / total[2:3], rho_p / total[3:4])
    res_one = first_res - step_one * image_one
    precond = polw[...] * res_one
    sums = reduce_start(1, (res_one * precond,))
    halo_pairs(1, vhalo2, 0, cuts[2], cuts[3])
    sums = reduce_middle(1, sums)
    halo_pairs(1, vhalo2, 0, cuts[3], cuts[5])
    backs = send_back(1)
    started.extend(backs)
    off_pairs(1, vrow2, 0)
    mutual = own_field()
    total = reduce_end(1, sums)
    next_d, next_p = total[0:1], total[1:2]
    ratio = spread_sets(next_d / rho_d, next_p / rho_p)
    for s in range(4):
        backs[s].wait_recv()
        mutual = mutual + back_in[1, s]
    image_vec = vec_two / polw[...] - mutual * maskw[...]
    search_two = precond + ratio * search
    image_two = (image_one - step_one * image_vec) + ratio * image_one
    sums = reduce_start(2, (search_two * image_two,))
    sums = reduce_middle(2, sums)
    total = reduce_end(2, sums)
    step_two = spread_sets(next_d / total[0:1], next_p / total[1:2])
    resid[...] = step_one * search + step_two * search_two
    image[...] = res_one - step_two * image_two
    for b in range(blocks):
        dip_ref[b] = resid[pl.ds(6 * b, 6), :]
        res_ref[b] = image[pl.ds(6 * b, 6), :]
    for copy in started:
        copy.wait_send()


def per_device(nx, ny, positions, polarity, direct_field, atom_count, pair_list, pair_count):
    blocks, atoms = positions.shape[2], positions.shape[4]
    groups = atoms // ROWS
    comps = 6 * blocks
    vrows = -(-comps // 8) * 8
    links = 3 * blocks - 2
    names = -(-5 * blocks * blocks // 8) * 8
    f32 = jnp.float32
    vmem = pl.BlockSpec(memory_space=pltpu.VMEM)
    smem = pl.BlockSpec(memory_space=pltpu.SMEM)
    out = jax.ShapeDtypeStruct((blocks, 6, atoms), f32)
    sem = pltpu.SemaphoreType.DMA
    dipoles, residual = pl.pallas_call(
        functools.partial(kernel, nx, ny, blocks),
        out_shape=(out, out),
        in_specs=[smem, smem, vmem, vmem, vmem, vmem],
        out_specs=(vmem, vmem),
        scratch_shapes=[
            pltpu.VMEM((GEO_ROWS + vrows, atoms), f32),
            pltpu.VMEM((4, GEO_ROWS, atoms), f32),
            pltpu.VMEM((vrows, atoms), f32),
            pltpu.VMEM((4, vrows, atoms), f32),
            pltpu.VMEM((4, GEO_ROWS + vrows, atoms), f32),
            pltpu.VMEM((vrows, atoms), f32),
            pltpu.VMEM((vrows, atoms), f32),
            pltpu.VMEM((vrows, atoms), f32),
            pltpu.VMEM((vrows, atoms), f32),
            pltpu.VMEM((names, atoms), f32),
            pltpu.VMEM((4 * blocks, atoms, atoms), f32),
            pltpu.VMEM((comps, atoms, atoms), f32),
            pltpu.VMEM((comps, atoms, atoms), f32),
            pltpu.VMEM((4, comps, 8, atoms), f32),
            pltpu.VMEM((comps, 8, atoms), f32),
            pltpu.VMEM((links * groups, 4, 4, ROWS, atoms), f32),
            pltpu.VMEM((blocks * groups, 4, ROWS, atoms), f32),
            pltpu.VMEM(((blocks - 1) * groups, 4, ROWS, atoms), f32),
            pltpu.VMEM((2, 4, vrows, atoms), f32),
            pltpu.VMEM((2, 4, vrows, atoms), f32),
            pltpu.VMEM((3, 2, 8, atoms), f32),
            pltpu.VMEM((3, nx - 1, 8, atoms), f32),
            pltpu.VMEM((3, ny - 1, 8, atoms), f32),
            sem((2, 4)),
            sem((2, 4)),
            sem((2, 4)),
            sem((2, 4)),
            sem((3, nx - 1)),
            sem((3, nx - 1)),
            sem((3, ny - 1)),
            sem((3, ny - 1)),
        ],
        compiler_params=pltpu.CompilerParams(
            collective_id=0, has_side_effects=True, vmem_limit_bytes=40 * 1024 * 1024
        ),
    )(
        atom_count[0],
        pair_count,
        positions[0, 0],
        polarity[0, 0],
        direct_field[0, 0],
        pair_list[0, 0],
    )
    return (dipoles[None, None], residual[None, None])


def solution(mesh):
    in_specs = (
        P("gx", "gy", None, None, None),
        P("gx", "gy", None, None),
        P("gx", "gy", None, None, None),
        P("gx", "gy", None),
        P("gx", "gy", None, None),
        P("gx", "gy"),
    )
    out_specs = (P("gx", "gy", None, None, None), P("gx", "gy", None, None, None))
    body = functools.partial(per_device, mesh.shape["gx"], mesh.shape["gy"])
    return jax.shard_map(
        body, mesh=mesh, in_specs=in_specs, out_specs=out_specs, check_vma=False
    )
```

time: 327 us -> 63.5 us (0.19); the launches traced: 321 us -> 63.1 us
  blocking collectives: 122 us -> 0 us
  waiting for transfers between devices: 74.1 us -> 0 us
  other arithmetic: 65.1 us -> 0 us
  Pallas kernels: 0 us -> 59.2 us
  local copies, waits for them, and re-layouts: 29.2 us -> 2.6 us
  starting transfers between devices: 19.1 us -> 0 us
  matrix products: 7.15 us -> 0 us
    psum x3 -> x0, blocking collectives: 122 us -> none  [global_sums(): return lax.psum(local_values, ('gx', 'gy'))]
    ppermute x12 -> x0, waiting for transfers between devices: 74.1 us -> none  [the longest x4 49.2 us: from_behind(): return lax.ppermute(value, axis, pairs)]
    pallas_call x0 -> x1, Pallas kernels: none -> 59.2 us  [per_device(): pl.pallas_call(functools.partial(kernel, nx, ny, blocks), out_shape=(out,...]
    reduce_sum x37 -> x0, other arithmetic: 47.9 us -> none  [the longest x20 45.1 us: tensor_apply(): jnp.sum(scaled * deltas[member] - coef_three * moments[member], axis=axis...]
    gather x40 -> x0, local copies, waits for them, and re-layouts: 22.6 us -> none  [the longest x10 5.75 us: one_turn(): jnp.take(geom_stack, source, axis=0)]
    ppermute x12 -> x0, starting transfers between devices: 19.1 us -> none  [the longest x4 18.7 us: padded_2(): lax.ppermute(head, axis, [((i + 1) % count, i) for i in range(count)])]
    convert_element_type x11 -> x0, other arithmetic: 7.23 us -> none  [the longest x10 6.51 us: one_turn(): (first_row + jnp.arange(pair_batch, dtype=jnp.int32) < pair_total).astype...]
    dot_general x20 -> x0, matrix products: 7.15 us -> none  [the longest x10 3.58 us: one_turn(): jnp.einsum('gt,gca->tca', to_other, backward, precision=lax.Precision.HIG...]
  transfers between devices with their start and end apart: 12 -> 0, of which waited for: 12 -> 0; matrix products, arithmetic and copies ran while one was open for 0% -> 0% of each run, Pallas kernels for 0% -> 0%
where the time goes in v1:
time: 63.5 us; the launch traced here: 63.1 us
  Pallas kernels  59.2 us (93%)
  local copies, waits for them, and re-layouts  2.6 us (4%)
  between operations  1.37 us (2%)
    pallas_call x1, Pallas kernels, per_device(): pl.pallas_call(functools.partial(kernel, nx, ny, blocks), out_shape=(out,...  59.2 us
    unnamed x16, local copies, waits for them, and re-layouts  2.6 us

profile of v1, /device:TPU:0, one launch (start us, length us, event | category | flops | bytes accessed | tf_op | source)
XLA Modules:
  0.0 63.1 jit_solution(3892963036642533577)
XLA Ops:
  0.6 0.0 copy-start.4
  0.6 0.0 copy-start.3
  1.3 0.0 copy-start.2
  1.3 0.0 copy-done.4
  1.3 0.0 copy-start.1
  1.4 0.0 copy-done.3
  1.4 0.6 %copy-done.2 = f32[1,1,5,3,128]{4,1,3,2,0:T(1,128)S(1)} copy-done((f32[1,1,5,3,128]{4,1,3,2,0:T(1,128)S(1)}, f32[1,1,5,3,128]{4,1,3,2,0:T(1,128)}, u32[]{:S(2)}) %copy-start.2) | copy-done | bytes 7704
  2.0 0.0 copy-done.1
  2.1 0.0 copy-start
  2.1 0.7 %copy-done = s32[1,1,5]{2,1,0:T(1,128)S(1)} copy-done((s32[1,1,5]{2,1,0:T(1,128)S(1)}, s32[1,1,5]{2,1,0:T(1,128)}, u32[]{:S(2)}) %copy-start) | copy-done | bytes 44
  2.7 59.2 %shard_map.77 = (f32[5,6,128]{2,1,0:T(8,128)S(1)}, f32[5,6,128]{2,1,0:T(8,128)S(1)}) custom-call(s32[1,5]{1,0:T(1,128)S(1)} %bitcast.21, s32[1,1]{1,0:T(1,128)S(6)} %copy.22.total_ref, f32[5,3,128]{2,1,0:T(4,128)S(1)} %bitcast.16, f32[5,128]{1,0:T(8,128)S(1)} %bitcast.19, f32[5,6,128]{2,1,0:T(8,128)S(1)} %bitcast.15, s32[3,61]{1,0:T(4,128)S(1)} %bitcast.20), custom_call_target="tpu_custom_call" | custom-call | tf_op jit(solution)/shard_map/pallas_call | solution.py:419
  61.9 0.6 copy.8
  62.5 0.6 copy.9
  (4 shorter events, 0.0 us)
Async XLA Ops:
  0.6 0.7 %copy-start.4 = (s32[1,1,3,61]{3,1,2,0:T(1,128)S(1)}, s32[1,1,3,61]{3,1,2,0:T(1,128)}, u32[]{:S(2)}) copy-start(s32[1,1,3,61]{3,1,2,0:T(1,128)} %param.10) | copy-start | bytes 2200
  0.6 0.7 %copy-start.3 = (f32[1,1,5,128]{3,1,2,0:T(1,128)S(1)}, f32[1,1,5,128]{3,1,2,0:T(1,128)}, u32[]{:S(2)}) copy-start(f32[1,1,5,128]{3,1,2,0:T(1,128)} %param.7) | copy-start | bytes 7684
  1.3 0.7 %copy-start.2 = (f32[1,1,5,3,128]{4,1,3,2,0:T(1,128)S(1)}, f32[1,1,5,3,128]{4,1,3,2,0:T(1,128)}, u32[]{:S(2)}) copy-start(f32[1,1,5,3,128]{4,1,3,2,0:T(1,128)} %param.6) | copy-start | bytes 23044
  1.3 0.7 %copy-start.1 = (f32[1,1,5,6,128]{4,1,3,2,0:T(1,128)S(1)}, f32[1,1,5,6,128]{4,1,3,2,0:T(1,128)}, u32[]{:S(2)}) copy-start(f32[1,1,5,6,128]{4,1,3,2,0:T(1,128)} %param.8) | copy-start | bytes 46084
  2.1 0.7 %copy-start = (s32[1,1,5]{2,1,0:T(1,128)S(1)}, s32[1,1,5]{2,1,0:T(1,128)}, u32[]{:S(2)}) copy-start(s32[1,1,5]{2,1,0:T(1,128)} %param.9) | copy-start | bytes 64

commit v2 on v1

--- a/solution.py
+++ b/solution.py
@@ -12,6 +12,7 @@
 slot_moves = ((0, 1), (1, -1), (1, 0), (1, 1))
 GEO_ROWS = 24
 ROWS = 16
+slot_order = (2, 0, 1, 3)
 MESH = pl.DeviceIdType.MESH
 
 
@@ -61,6 +62,7 @@
 ):
     atoms = pos_ref.shape[2]
     groups = atoms // ROWS
+    links = 3 * blocks - 2
     comps = 6 * blocks
     vrows = polw.shape[0]
     me_x, me_y = lax.axis_index("gx"), lax.axis_index("gy")
@@ -92,11 +94,12 @@
         polw[pl.ds(6 * b, 6), :] = jnp.broadcast_to(pol, (6, atoms))
         maskw[pl.ds(6 * b, 6), :] = jnp.broadcast_to(mask, (6, atoms))
 
-    pl.semaphore_wait(barrier, len(partners))
+    started = []
 
     def send_mail(turn, source, target):
-        copies = []
-        for s, (dx, dy) in enumerate(slot_moves):
+        copies = {}
+        for s in slot_order:
+            dx, dy = slot_moves[s]
             copy = pltpu.make_async_remote_copy(
                 src_ref=source,
                 dst_ref=target.at[s],
@@ -106,24 +109,23 @@
                 device_id_type=MESH,
             )
             copy.start()
-            copies.append(copy)
+            started.append(copy)
+            copies[s] = copy
         return copies
 
-    def send_back(turn):
-        copies = []
-        for s, (dx, dy) in enumerate(slot_moves):
-            back_out[turn, s, pl.ds(0, comps), :] = jnp.sum(bacc[s], axis=1)
-            copy = pltpu.make_async_remote_copy(
-                src_ref=back_out.at[turn, s],
-                dst_ref=back_in.at[turn, s],
-                send_sem=back_ss.at[turn, s],
-                recv_sem=back_rs.at[turn, s],
-                device_id=device(dx, dy),
-                device_id_type=MESH,
-            )
-            copy.start()
-            copies.append(copy)
-        return copies
+    def send_back(turn, s):
+        back_out[turn, s, pl.ds(0, comps), :] = jnp.sum(bacc[s], axis=1)
+        copy = pltpu.make_async_remote_copy(
+            src_ref=back_out.at[turn, s],
+            dst_ref=back_in.at[turn, s],
+            send_sem=back_ss.at[turn, s],
+            recv_sem=back_rs.at[turn, s],
+            device_id=device(*slot_moves[s]),
+            device_id_type=MESH,
+        )
+        copy.start()
+        started.append(copy)
+        return copy
 
     def spread_x(turn):
         copies = []
@@ -155,7 +157,6 @@
             copies.append(copy)
         return copies
 
-    started = []
     row_id = lax.broadcasted_iota(jnp.int32, (vrows, atoms), 0)
     in_set_d = lax.rem(row_id, 6) < 3
 
@@ -279,35 +280,37 @@
 
         lax.fori_loop(0, (blocks - 1) * groups, step, 0)
 
-    def halo_pairs(turn, vhalo, voff, first, last):
+    def halo_pairs(turn, s, vhalo, voff):
+        chunk = 2 if groups % 2 == 0 else 1
+
         def step(n, carry):
-            k, g = n // groups, lax.rem(n, groups)
+            k, part = n // (groups // chunk), lax.rem(n, groups // chunk)
             b = (k + 1) // 3
             c = k - 2 * b
-            vi = own_part(vb, 6 * b, g, 6)
+            vj = [vhalo[s, pl.ds(voff + 6 * c + m, 1), :] for m in range(6)]
             if turn == 0:
-                own = own_part(gb, 4 * b, g, 4)
-            total = None
-            for s in range(4):
+                keep = weight[pl.ds((s + 1) * blocks * blocks + b * blocks + c, 1), :]
+                other = [geo[s, pl.ds(4 * c + m, 1), :] for m in range(4)]
+            back = None
+            for h in range(chunk):
+                g = part * chunk + h
+                at = k * groups + g
                 if turn == 0:
-                    keep = weight[pl.ds((s + 1) * blocks * blocks + b * blocks + c, 1), :]
-                    other = [geo[s, pl.ds(4 * c + m, 1), :] for m in range(4)]
-                    t = tensor(own, other, keep, None)
+                    t = tensor(own_part(gb, 4 * b, g, 4), other, keep, None)
                     for m in range(4):
-                        tens[n, s, m] = t[m]
+                        tens[at, s, m] = t[m]
                 else:
-                    t = [tens[n, s, m] for m in range(4)]
-                vj = [vhalo[s, pl.ds(voff + 6 * c + m, 1), :] for m in range(6)]
+                    t = [tens[at, s, m] for m in range(4)]
                 out = apply(t, vj)
-                total = out if total is None else [p + q for p, q in zip(total, out)]
-                ret = apply(t, vi)
                 for m in range(6):
-                    bacc[s, 6 * c + m] += fold(ret[m])
+                    fa[6 * b + m, pl.ds(g * ROWS, ROWS), :] += out[m]
+                ret = [fold(r) for r in apply(t, own_part(vb, 6 * b, g, 6))]
+                back = ret if back is None else [p + q for p, q in zip(back, ret)]
             for m in range(6):
-                fa[6 * b + m, pl.ds(g * ROWS, ROWS), :] += total[m]
+                bacc[s, 6 * c + m] += back[m]
             return carry
 
-        lax.fori_loop(first * groups, last * groups, step, 0)
+        lax.fori_loop(0, links * (groups // chunk), step, 0)
 
     lane_sq = lax.broadcasted_iota(jnp.int32, (atoms, atoms), 1)
 
@@ -319,12 +322,10 @@
         image[pl.ds(0, comps), :] = jnp.sum(bown[...], axis=1)
         return square.T[0:vrows] + image[...]
 
-    links = 3 * blocks - 2
     own_vec = mail.at[pl.ds(GEO_ROWS, vrows)]
 
-    mails = send_mail(0, mail, gmail)
-    started.extend(mails)
     back_out[...] = jnp.zeros_like(back_out)
+    bacc[...] = jnp.zeros_like(bacc)
     search = own_vec[...]
     first_res = resid[...]
     broadcast_rows(mail[pl.ds(0, GEO_ROWS), :], gb, 4 * blocks)
@@ -337,20 +338,22 @@
     found = jnp.sum((names == code).astype(jnp.float32), axis=1, keepdims=True)
     weight[...] = jnp.broadcast_to(found, weight.shape)
 
-    bacc[...] = jnp.zeros_like(bacc)
+    pl.semaphore_wait(barrier, len(partners))
+    mails = send_mail(0, mail, gmail)
     diag_pairs(0, mail, GEO_ROWS)
     geo_row = lax.rem(lax.broadcasted_iota(jnp.int32, (GEO_ROWS, atoms), 0), 4)
-    for s, (dx, dy) in enumerate(slot_moves):
+    backs = {}
+    for s in slot_order:
+        dx, dy = slot_moves[s]
         mails[s].wait_recv()
         shift = jnp.where(geo_row == 0, column_width * dx, 0.0)
         shift = jnp.where(geo_row == 1, column_width * dy, shift)
         geo[s] = gmail[s, pl.ds(0, GEO_ROWS), :] + shift
-    halo_pairs(0, gmail, GEO_ROWS, 0, links)
-    backs = send_back(0)
-    started.extend(backs)
+        halo_pairs(0, s, gmail, GEO_ROWS)
+        backs[s] = send_back(0, s)
     off_pairs(0, mail, GEO_ROWS)
     mutual = own_field()
-    for s in range(4):
+    for s in slot_order:
         backs[s].wait_recv()
         mutual = mutual + back_in[0, s]
     image_one = search / polw[...] - mutual * maskw[...]
@@ -358,41 +361,47 @@
     vrow2[...] = vec_two
 
     mails = send_mail(1, vrow2, vhalo2)
-    started.extend(mails)
     sums = reduce_start(0, (first_res * search, search * image_one))
     broadcast_rows(vec_two, vb, comps)
     bacc[...] = jnp.zeros_like(bacc)
     diag_pairs(1, vrow2, 0)
-    for s in range(4):
+    for place, s in enumerate(slot_order):
         mails[s].wait_recv()
-    cuts = [links * i // 5 for i in range(6)]
-    halo_pairs(1, vhalo2, 0, cuts[0], cuts[1])
-    sums = reduce_middle(0, sums)
-    halo_pairs(1, vhalo2, 0, cuts[1], cuts[2])
-    total = reduce_end(0, sums)
-    rho_d, rho_p = total[0:1], total[1:2]
-    step_one = spread_sets(rho_d / total[2:3], rho_p / total[3:4])
-    res_one = first_res - step_one * image_one
-    precond = polw[...] * res_one
-    sums = reduce_start(1, (res_one * precond,))
-    halo_pairs(1, vhalo2, 0, cuts[2], cuts[3])
-    sums = reduce_middle(1, sums)
-    halo_pairs(1, vhalo2, 0, cuts[3], cuts[5])
-    backs = send_back(1)
-    started.extend(backs)
+        halo_pairs(1, s, vhalo2, 0)
+        backs[s] = send_back(1, s)
+        if place == 0:
+            sums = reduce_middle(0, sums)
+        elif place == 1:
+            total = reduce_end(0, sums)
+            rho_d, rho_p = total[0:1], total[1:2]
+            step_one = spread_sets(rho_d / total[2:3], rho_p / total[3:4])
+            res_one = first_res - step_one * image_one
+            precond = polw[...] * res_one
+            sums = reduce_start(1, (res_one * precond,))
+        elif place == 2:
+            sums = reduce_middle(1, sums)
     off_pairs(1, vrow2, 0)
     mutual = own_field()
     total = reduce_end(1, sums)
     next_d, next_p = total[0:1], total[1:2]
     ratio = spread_sets(next_d / rho_d, next_p / rho_p)
+    search_two = precond + ratio * search
+    own_image = vec_two / polw[...]
+    product = search_two * mutual
     for s in range(4):
+        start = gmail[s, pl.ds(GEO_ROWS, vrows), :]
+        halo_two = (start - step_one * vhalo2[s]) + ratio * start
+        product = product + halo_two * back_out[1, s]
+    product = step_one * product + search_two * (
+        (image_one - step_one * own_image) + ratio * image_one
+    )
+    sums = reduce_start(2, (product,))
+    sums = reduce_middle(2, sums)
+    for s in slot_order:
         backs[s].wait_recv()
         mutual = mutual + back_in[1, s]
-    image_vec = vec_two / polw[...] - mutual * maskw[...]
-    search_two = precond + ratio * search
+    image_vec = own_image - mutual * maskw[...]
     image_two = (image_one - step_one * image_vec) + ratio * image_one
-    sums = reduce_start(2, (search_two * image_two,))
-    sums = reduce_middle(2, sums)
     total = reduce_end(2, sums)
     step_two = spread_sets(next_d / total[0:1], next_p / total[1:2])
     resid[...] = step_one * search + step_two * search_two

time: 63.5 us -> 61.4 us (0.967)
  Pallas kernels: 59.2 us -> 57.1 us
    pallas_call x1, Pallas kernels: 59.2 us -> 57.1 us  [per_device(): pl.pallas_call(functools.partial(kernel, nx, ny, blocks), out_shape=(out,...]
where the time goes in v2:
time: 61.4 us; the launch traced here: 61 us
  Pallas kernels  57.1 us (93%)
  local copies, waits for them, and re-layouts  2.6 us (4%)
  between operations  1.37 us (2%)
    pallas_call x1, Pallas kernels, per_device(): pl.pallas_call(functools.partial(kernel, nx, ny, blocks), out_shape=(out,...  57.1 us
    unnamed x16, local copies, waits for them, and re-layouts  2.6 us

profile of v2, /device:TPU:0, one launch (start us, length us, event | category | flops | bytes accessed | tf_op | source)
XLA Modules:
  0.0 61.0 jit_solution(15330552365530213044)
XLA Ops:
  0.6 0.0 copy-start.4
  0.6 0.0 copy-start.3
  1.3 0.0 copy-start.2
  1.3 0.0 copy-done.4
  1.3 0.0 copy-start.1
  1.4 0.0 copy-done.3
  1.4 0.6 %copy-done.2 = f32[1,1,5,3,128]{4,1,3,2,0:T(1,128)S(1)} copy-done((f32[1,1,5,3,128]{4,1,3,2,0:T(1,128)S(1)}, f32[1,1,5,3,128]{4,1,3,2,0:T(1,128)}, u32[]{:S(2)}) %copy-start.2) | copy-done | bytes 7704
  2.0 0.0 copy-done.1
  2.1 0.0 copy-start
  2.1 0.7 %copy-done = s32[1,1,5]{2,1,0:T(1,128)S(1)} copy-done((s32[1,1,5]{2,1,0:T(1,128)S(1)}, s32[1,1,5]{2,1,0:T(1,128)}, u32[]{:S(2)}) %copy-start) | copy-done | bytes 44
  2.7 57.1 %shard_map.77 = (f32[5,6,128]{2,1,0:T(8,128)S(1)}, f32[5,6,128]{2,1,0:T(8,128)S(1)}) custom-call(s32[1,5]{1,0:T(1,128)S(1)} %bitcast.21, s32[1,1]{1,0:T(1,128)S(6)} %copy.22.total_ref, f32[5,3,128]{2,1,0:T(4,128)S(1)} %bitcast.16, f32[5,128]{1,0:T(8,128)S(1)} %bitcast.19, f32[5,6,128]{2,1,0:T(8,128)S(1)} %bitcast.15, s32[3,61]{1,0:T(4,128)S(1)} %bitcast.20), custom_call_target="tpu_custom_call" | custom-call | tf_op jit(solution)/shard_map/pallas_call | solution.py:428
  59.8 0.6 %copy.8 = f32[1,1,5,6,128]{4,1,3,2,0:T(1,128)} copy(f32[1,1,5,6,128]{4,3,2,1,0:T(8,128)S(1)} %bitcast.18) | data formatting | bytes 30720
  60.4 0.6 %copy.9 = f32[1,1,5,6,128]{4,1,3,2,0:T(1,128)} copy(f32[1,1,5,6,128]{4,3,2,1,0:T(8,128)S(1)} %bitcast.17) | data formatting | bytes 30720
  (4 shorter events, 0.0 us)
Async XLA Ops:
  0.6 0.7 %copy-start.4 = (s32[1,1,3,61]{3,1,2,0:T(1,128)S(1)}, s32[1,1,3,61]{3,1,2,0:T(1,128)}, u32[]{:S(2)}) copy-start(s32[1,1,3,61]{3,1,2,0:T(1,128)} %param.10) | copy-start | bytes 2200
  0.6 0.7 %copy-start.3 = (f32[1,1,5,128]{3,1,2,0:T(1,128)S(1)}, f32[1,1,5,128]{3,1,2,0:T(1,128)}, u32[]{:S(2)}) copy-start(f32[1,1,5,128]{3,1,2,0:T(1,128)} %param.7) | copy-start | bytes 7684
  1.3 0.7 %copy-start.2 = (f32[1,1,5,3,128]{4,1,3,2,0:T(1,128)S(1)}, f32[1,1,5,3,128]{4,1,3,2,0:T(1,128)}, u32[]{:S(2)}) copy-start(f32[1,1,5,3,128]{4,1,3,2,0:T(1,128)} %param.6) | copy-start | bytes 23044
  1.3 0.7 %copy-start.1 = (f32[1,1,5,6,128]{4,1,3,2,0:T(1,128)S(1)}, f32[1,1,5,6,128]{4,1,3,2,0:T(1,128)}, u32[]{:S(2)}) copy-start(f32[1,1,5,6,128]{4,1,3,2,0:T(1,128)} %param.8) | copy-start | bytes 46084
  2.1 0.7 %copy-start = (s32[1,1,5]{2,1,0:T(1,128)S(1)}, s32[1,1,5]{2,1,0:T(1,128)}, u32[]{:S(2)}) copy-start(s32[1,1,5]{2,1,0:T(1,128)} %param.9) | copy-start | bytes 64

commit v3 on v2

--- a/solution.py
+++ b/solution.py
@@ -11,7 +11,7 @@
 column_width = 8.0
 slot_moves = ((0, 1), (1, -1), (1, 0), (1, 1))
 GEO_ROWS = 24
-ROWS = 16
+ROWS = 32
 slot_order = (2, 0, 1, 3)
 MESH = pl.DeviceIdType.MESH
 
@@ -230,7 +230,7 @@
         return out
 
     def fold(x):
-        return x[0:8] + x[8:16]
+        return jnp.sum(x.reshape(ROWS // 8, 8, atoms), axis=0)
 
     def rows_of(ref, first, count):
         return [ref[pl.ds(first + m, 1), :] for m in range(count)]
@@ -281,7 +281,7 @@
         lax.fori_loop(0, (blocks - 1) * groups, step, 0)
 
     def halo_pairs(turn, s, vhalo, voff):
-        chunk = 2 if groups % 2 == 0 else 1
+        chunk = 4 if groups % 4 == 0 else 1
 
         def step(n, carry):
             k, part = n // (groups // chunk), lax.rem(n, groups // chunk)

time: 61.4 us -> 53 us (0.86)
  Pallas kernels: 57.1 us -> 48.7 us
    pallas_call x1, Pallas kernels: 57.1 us -> 48.7 us  [per_device(): pl.pallas_call(functools.partial(kernel, nx, ny, blocks), out_shape=(out,...]
where the time goes in v3:
time: 53 us; the launch traced here: 52.7 us
  Pallas kernels  48.7 us (92%)
  local copies, waits for them, and re-layouts  2.6 us (5%)
  between operations  1.37 us (3%)
    pallas_call x1, Pallas kernels, per_device(): pl.pallas_call(functools.partial(kernel, nx, ny, blocks), out_shape=(out,...  48.7 us
    unnamed x16, local copies, waits for them, and re-layouts  2.6 us

profile of v3, /device:TPU:0, one launch (start us, length us, event | category | flops | bytes accessed | tf_op | source)
XLA Modules:
  0.0 52.7 jit_solution(16547699747961530867)
XLA Ops:
  0.6 0.0 copy-start.4
  0.6 0.0 copy-start.3
  1.3 0.0 copy-start.2
  1.3 0.0 copy-done.4
  1.3 0.0 copy-start.1
  1.4 0.0 copy-done.3
  1.4 0.6 %copy-done.2 = f32[1,1,5,3,128]{4,1,3,2,0:T(1,128)S(1)} copy-done((f32[1,1,5,3,128]{4,1,3,2,0:T(1,128)S(1)}, f32[1,1,5,3,128]{4,1,3,2,0:T(1,128)}, u32[]{:S(2)}) %copy-start.2) | copy-done | bytes 7704
  2.0 0.0 copy-done.1
  2.1 0.0 copy-start
  2.1 0.7 %copy-done = s32[1,1,5]{2,1,0:T(1,128)S(1)} copy-done((s32[1,1,5]{2,1,0:T(1,128)S(1)}, s32[1,1,5]{2,1,0:T(1,128)}, u32[]{:S(2)}) %copy-start) | copy-done | bytes 44
  2.7 48.7 %shard_map.77 = (f32[5,6,128]{2,1,0:T(8,128)S(1)}, f32[5,6,128]{2,1,0:T(8,128)S(1)}) custom-call(s32[1,5]{1,0:T(1,128)S(1)} %bitcast.21, s32[1,1]{1,0:T(1,128)S(6)} %copy.22.total_ref, f32[5,3,128]{2,1,0:T(4,128)S(1)} %bitcast.16, f32[5,128]{1,0:T(8,128)S(1)} %bitcast.19, f32[5,6,128]{2,1,0:T(8,128)S(1)} %bitcast.15, s32[3,61]{1,0:T(4,128)S(1)} %bitcast.20), custom_call_target="tpu_custom_call" | custom-call | tf_op jit(solution)/shard_map/pallas_call | solution.py:428
  51.4 0.6 %copy.8 = f32[1,1,5,6,128]{4,1,3,2,0:T(1,128)} copy(f32[1,1,5,6,128]{4,3,2,1,0:T(8,128)S(1)} %bitcast.18) | data formatting | bytes 30720
  52.1 0.6 %copy.9 = f32[1,1,5,6,128]{4,1,3,2,0:T(1,128)} copy(f32[1,1,5,6,128]{4,3,2,1,0:T(8,128)S(1)} %bitcast.17) | data formatting | bytes 30720
  (4 shorter events, 0.0 us)
Async XLA Ops:
  0.6 0.7 %copy-start.4 = (s32[1,1,3,61]{3,1,2,0:T(1,128)S(1)}, s32[1,1,3,61]{3,1,2,0:T(1,128)}, u32[]{:S(2)}) copy-start(s32[1,1,3,61]{3,1,2,0:T(1,128)} %param.10) | copy-start | bytes 2200
  0.6 0.7 %copy-start.3 = (f32[1,1,5,128]{3,1,2,0:T(1,128)S(1)}, f32[1,1,5,128]{3,1,2,0:T(1,128)}, u32[]{:S(2)}) copy-start(f32[1,1,5,128]{3,1,2,0:T(1,128)} %param.7) | copy-start | bytes 7684
  1.3 0.7 %copy-start.2 = (f32[1,1,5,3,128]{4,1,3,2,0:T(1,128)S(1)}, f32[1,1,5,3,128]{4,1,3,2,0:T(1,128)}, u32[]{:S(2)}) copy-start(f32[1,1,5,3,128]{4,1,3,2,0:T(1,128)} %param.6) | copy-start | bytes 23044
  1.3 0.7 %copy-start.1 = (f32[1,1,5,6,128]{4,1,3,2,0:T(1,128)S(1)}, f32[1,1,5,6,128]{4,1,3,2,0:T(1,128)}, u32[]{:S(2)}) copy-start(f32[1,1,5,6,128]{4,1,3,2,0:T(1,128)} %param.8) | copy-start | bytes 46084
  2.1 0.7 %copy-start = (s32[1,1,5]{2,1,0:T(1,128)S(1)}, s32[1,1,5]{2,1,0:T(1,128)}, u32[]{:S(2)}) copy-start(s32[1,1,5]{2,1,0:T(1,128)} %param.9) | copy-start | bytes 64
